TPU v7x, 256 devices: a whole 4x4x8 slice. The times are simulated.
256 devices in a mesh: group: 8 (over z), block: 32 (over x, y, core).
Axes of the slice: x: 4, y: 4, z: 8, core: 2. Of those that a mesh axis runs over, the one named last changes fastest.
Arguments:
- jacobians: bfloat16 [3072, 128, 1152], P(('group', 'block')), may hold values from -0.15625 to 0.15625
- destination: int32 [3072], P(('group', 'block')), may hold values from 0 to 31, as said below
- other_group: int32 [3072], P(('group', 'block')), may hold values from 0 to 7, as said below
- live_rows: int32 [3072], P(('group', 'block')), may hold values from 64 to 128, as said below
- damping: float32 [256, 576], P(('group', 'block')), may hold values from 0.5 to 2
- right_side: float32 [256, 576], P(('group', 'block')), may hold values from -18 to 18
Outputs:
- solution: float32 [256, 576], P(('group', 'block'))
- residual: float32 [256, 576], P(('group', 'block'))
Inputs may be any that keep to these rules, and one draw needn't show every extreme that they name: `destination`: the observation blocks of one device name any one camera block at most 2 times; in every group some camera block is named exactly 2 times by every device of that group. `other_group`: an observation block's covisible group differs from the group of the device that holds it. `live_rows`: every device holds a block whose 128 rows are all live.
All inputs are finite; a program needn't handle non-finite values.
Results may differ from a plain program's by a relative error of at most 0.009.
Values may be sent and summed in bfloat16 or wider, within the bound.
A program may use at most 128 MiB of HBM per device.

v0:
```python
import jax
import jax.numpy as jnp
from jax import lax
from jax.sharding import PartitionSpec as P

ITERS = 2


def global_norm(residual, scaled_res):
    return lax.psum(jnp.sum(residual * scaled_res), ("group", "block"))


def on_device(jacobians, destination, other_group, live_rows, damping, right_side):
    block_count, row_count, block_width = jacobians.shape
    param_count = block_width // 2
    owners = lax.axis_size("block")
    groups = lax.axis_size("group")
    my_group = lax.axis_index("group")
    row_index = jnp.arange(row_count, dtype=jnp.int32)
    kept_blocks = jnp.where(
        row_index[None, :, None] < live_rows[:, None, None], jacobians, jnp.zeros_like(jacobians)
    )
    capacity = max(2, 2 * ((block_count + owners - 1) // owners))
    same_owner = destination[:, None] == destination[None, :]
    positions = jnp.arange(block_count, dtype=jnp.int32)
    before = positions[None, :] < positions[:, None]
    slot_rank = jnp.sum((same_owner & before).astype(jnp.int32), axis=1)
    slot_index = destination * capacity + slot_rank
    send_blocks = (
        jnp.zeros((owners * capacity, row_count, block_width), jnp.bfloat16)
        .at[slot_index]
        .set(kept_blocks)
    )
    send_groups = jnp.zeros((owners * capacity,), jnp.int32).at[slot_index].set(other_group)
    send_blocks = send_blocks.reshape(owners, capacity, row_count, block_width)
    send_groups = send_groups.reshape(owners, capacity)
    got_blocks, got_groups = (
        lax.all_to_all(send_blocks, "block", split_axis=0, concat_axis=0, tiled=True),
        lax.all_to_all(send_groups, "block", split_axis=0, concat_axis=0, tiled=True),
    )
    got_blocks = got_blocks.reshape(owners * capacity, row_count, block_width)
    got_groups = got_groups.reshape(owners * capacity)
    group_ids = jnp.arange(groups, dtype=jnp.int32)
    own_mask = (group_ids == my_group).astype(jnp.float32)
    selector = (got_groups[:, None] == group_ids[None, :]).astype(jnp.float32)
    selector_low = selector.astype(jnp.bfloat16)

    def spread(term_rows):
        home_total = jnp.sum(term_rows[:, :param_count], axis=0)
        far_total = jnp.dot(
            selector.T,
            term_rows[:, param_count:],
            precision=lax.Precision.HIGHEST,
            preferred_element_type=jnp.float32,
        )
        return far_total + own_mask[:, None] * home_total[None, :]

    squares = jnp.einsum("src,src->sc", got_blocks, got_blocks, preferred_element_type=jnp.float32)
    diagonal_sum = damping + lax.psum_scatter(
        spread(squares), "group", scatter_dimension=0, tiled=True
    )
    solution = jnp.zeros_like(right_side)
    residual = right_side
    scaled_res = residual / diagonal_sum
    direction = scaled_res
    precond_norm = global_norm(residual, scaled_res)
    for iteration in range(ITERS):
        low_field = direction.astype(jnp.bfloat16)
        panel_low = lax.all_gather(low_field, "group", axis=0, tiled=True)
        far_inputs = jnp.dot(selector_low, panel_low, preferred_element_type=jnp.float32).astype(
            jnp.bfloat16
        )
        near_inputs = jnp.broadcast_to(low_field, far_inputs.shape)
        inputs = jnp.concatenate([near_inputs, far_inputs], axis=1)
        projected = jnp.einsum(
            "src,sc->sr", got_blocks, inputs, preferred_element_type=jnp.float32
        ).astype(jnp.bfloat16)
        returned = jnp.einsum(
            "src,sr->sc", got_blocks, projected, preferred_element_type=jnp.float32
        )
        operator_image = damping * direction + lax.psum_scatter(
            spread(returned), "group", scatter_dimension=0, tiled=True
        )
        curvature = lax.psum(jnp.sum(direction * operator_image), ("group", "block"))
        step_size = precond_norm / curvature
        solution = solution + step_size * direction
        residual = residual - step_size * operator_image
        if iteration + 1 < ITERS:
            scaled_res = residual / diagonal_sum
            next_norm = global_norm(residual, scaled_res)
            direction = scaled_res + next_norm / precond_norm * direction
            precond_norm = next_norm
    return (solution, residual)


def solution(mesh):
    placed = (
        P(("group", "block"), None, None),
        P(("group", "block")),
        P(("group", "block")),
        P(("group", "block")),
        P(("group", "block"), None),
        P(("group", "block"), None),
    )
    return jax.shard_map(
        on_device,
        mesh=mesh,
        in_specs=placed,
        out_specs=(P(("group", "block"), None), P(("group", "block"), None)),
        check_vma=False,
    )
```

profile of v0, /device:TPU:1, one launch (start us, length us, event | category | flops | bytes accessed | tf_op | source)
XLA Modules:
  0.0 751.9 jit_solution(11086218036957085777)
XLA Ops:
  0.6 0.9 convert_reduce_fusion
  3.7 8.6 %all-to-all-start = ((s32[32,1,2]{2,1,0:T(1,128)}), s32[32,1,2]{2,1,0:T(1,128)S(1)}, u32[]{:S(2)}, u32[]{:S(2)}) async-start(s32[32,1,2]{2,1,0:T(1,128)} %bitcast.2), calls=%async_computation | async-start | bytes 32768 | tf_op jit(solution)/shard_map/all_to_all | solution.py:39
  13.0 2.3 broadcast_select_fusion
  15.3 7.1 broadcast_in_dim.26
  22.4 7.7 %scatter_fusion = bf16[64,128,1152]{2,1,0:T(8,128)(2,1)} fusion(bf16[64,128,1152]{2,1,0:T(8,128)(2,1)} %broadcast_in_dim.26, s32[12]{0:T(128)} %copy-done.2, bf16[12,128,1152]{2,1,0:T(8,128)(2,1)S(1)} %broadcast_select_fusion), kind=kCustom, calls=%fused_computation.1 | custom fusion | bytes 10616880 | tf_op jit(solution)/shard_map/scatter | solution.py:32
  30.2 7.5 %all-to-all-start.1 = ((bf16[32,2,128,1152]{3,2,1,0:T(8,128)(2,1)}), bf16[32,2,128,1152]{3,2,1,0:T(8,128)(2,1)}, u32[]{:S(2)}, u32[]{:S(2)}) async-start(bf16[32,2,128,1152]{3,2,1,0:T(8,128)(2,1)} %bitcast.41), calls=%async_computation.1 | async-start | bytes 37748736 | tf_op jit(solution)/shard_map/all_to_all | solution.py:38
  39.6 261.2 %all-to-all-done.1 = bf16[32,2,128,1152]{3,2,1,0:T(8,128)(2,1)} async-done(((bf16[32,2,128,1152]{3,2,1,0:T(8,128)(2,1)}), bf16[32,2,128,1152]{3,2,1,0:T(8,128)(2,1)}, u32[]{:S(2)}, u32[]{:S(2)}) %all-to-all-start.1) | async-done | bytes 18874400 | tf_op jit(solution)/shard_map/all_to_all | solution.py:38
  300.8 8.3 %fusion = f32[64,1152]{1,0:T(8,128)S(1)} fusion(bf16[32,2,128,1152]{3,2,1,0:T(8,128)(2,1)} %all-to-all-done.1), kind=kLoop, calls=%fused_computation.3 | loop fusion | flops 28237824 | bytes 19169280 | tf_op jit(solution)/shard_map/src,src->sc/dot_general | solution.py:58
  309.4 25.5 %all-reduce = f32[8,576]{1,0:T(8,128)S(1)} all-reduce(f32[8,576]{1,0:T(8,128)S(1)} %convolution_add_fusion.2), channel_id=2, replica_groups=mesh['group'=8,'block'=32] {'group'}, use_global_device_ids=true, to_apply=%region_4.5.clone | all-reduce | flops 4608 | bytes 36864
  335.6 18.1 %all-gather = bf16[8,1,576]{2,1,0:T(2,128)(2,1)S(1)} all-gather(bf16[1,1,576]{2,1,0:T(2,128)(2,1)S(1)} %convert_bitcast_fusion.3), channel_id=1, replica_groups=mesh['group'=8,'block'=32] {'group'}, dimensions={0}, use_global_device_ids=true | all-gather | bytes 10368 | tf_op jit(solution)/shard_map/all_gather | solution.py:69
  354.0 10.1 %fusion.3 = f32[64,1,128]{2,1,0:T(1,128)S(1)} fusion(bf16[64,128,1152]{2,1,0:T(8,128)(2,1)} %bitcast.4, bf16[64,1152,1]{1,0,2:T(8,128)(2,1)S(1)} %maximum_bitcast_fusion), kind=kOutput, calls=%fused_computation.14 | convolution fusion | flops 18874368 | bytes 19054592 | tf_op jit(solution)/shard_map/src,sc->sr/dot_general | solution.py:75
  364.2 7.8 %fusion.10 = f32[64,1,1152]{2,1,0:T(1,128)S(1)} fusion(bf16[64,128,1152]{2,1,0:T(8,128)(2,1)} %bitcast.4, bf16[64,128,1]{1,0,2:T(8,128)(2,1)S(1)} %convert_bitcast_fusion.1), kind=kOutput, calls=%fused_computation.26 | convolution fusion | flops 18874368 | bytes 19185664 | tf_op jit(solution)/shard_map/src,sr->sc/dot_general | solution.py:78
  372.4 20.1 %all-reduce.1 = f32[8,576]{1,0:T(8,128)S(1)} all-reduce(f32[8,576]{1,0:T(8,128)S(1)} %convolution_add_fusion.1), channel_id=3, replica_groups=mesh['group'=8,'block'=32] {'group'}, use_global_device_ids=true, to_apply=%region_8.9.clone | all-reduce | flops 4608 | bytes 36864
  392.5 1.2 multiply_reduce_fusion.2
  393.7 133.7 %all-reduce.3 = (f32[]{:T(128)}, f32[]{:T(128)}) all-reduce(f32[]{:T(128)} %get-tuple-element.3, f32[]{:T(128)} %get-tuple-element.2), channel_id=1, replica_groups=mesh['group'=8,'block'=32] {'group','block'}, use_global_device_ids=true, to_apply=%region_6.7 | all-reduce | flops 2 | bytes 16 | tf_op jit(solution)/shard_map/psum | solution.py:10
  528.7 1.2 multiply_reduce_fusion.1
  530.0 73.4 %psum.30 = f32[]{:T(128)} all-reduce(f32[]{:T(128)} %get-tuple-element.8), channel_id=1, replica_groups=mesh['group'=8,'block'=32] {'group','block'}, use_global_device_ids=true, to_apply=%region_12.13 | all-reduce | flops 1 | bytes 8 | tf_op jit(solution)/shard_map/psum | solution.py:10
  604.8 17.9 %all-gather.1 = bf16[8,1,576]{2,1,0:T(2,128)(2,1)S(1)} all-gather(bf16[1,1,576]{2,1,0:T(2,128)(2,1)S(1)} %convert_bitcast_fusion.2), channel_id=1, replica_groups=mesh['group'=8,'block'=32] {'group'}, dimensions={0}, use_global_device_ids=true | all-gather | bytes 10368 | tf_op jit(solution)/shard_map/all_gather | solution.py:69
  623.0 10.1 %fusion.1 = f32[64,1,128]{2,1,0:T(1,128)S(1)} fusion(bf16[64,128,1152]{2,1,0:T(8,128)(2,1)} %bitcast.4, bf16[64,1152,1]{1,0,2:T(8,128)(2,1)S(1)} %maximum_bitcast_fusion.1), kind=kOutput, calls=%fused_computation.11 | convolution fusion | flops 18874368 | bytes 19054592 | tf_op jit(solution)/shard_map/src,sc->sr/dot_general | solution.py:75
  633.2 7.8 %fusion.8 = f32[64,1,1152]{2,1,0:T(1,128)S(1)} fusion(bf16[64,128,1152]{2,1,0:T(8,128)(2,1)} %bitcast.4, bf16[64,128,1]{1,0,2:T(8,128)(2,1)S(1)} %convert_bitcast_fusion), kind=kOutput, calls=%fused_computation.24 | convolution fusion | flops 18874368 | bytes 19185664 | tf_op jit(solution)/shard_map/src,sr->sc/dot_general | solution.py:78
  641.4 20.9 %all-reduce.2 = f32[8,576]{1,0:T(8,128)S(1)} all-reduce(f32[8,576]{1,0:T(8,128)S(1)} %convolution_add_fusion), channel_id=4, replica_groups=mesh['group'=8,'block'=32] {'group'}, use_global_device_ids=true, to_apply=%region_14.15.clone | all-reduce | flops 4608 | bytes 36864
  662.3 1.2 multiply_reduce_fusion
  663.5 85.8 %psum.31 = f32[]{:T(128)} all-reduce(f32[]{:T(128)} %multiply_reduce_fusion), channel_id=1, replica_groups=mesh['group'=8,'block'=32] {'group','block'}, use_global_device_ids=true, to_apply=%region_16.17 | all-reduce | flops 1 | bytes 8 | tf_op jit(solution)/shard_map/psum | solution.py:84
  750.7 1.2 multiply_subtract_fusion
  (38 shorter events, 7.0 us)
Async XLA Ops:
  2.2 10.0 %copy-start.2 = (s32[12]{0:T(128)}, s32[12]{0:T(128)S(1)}, u32[]{:S(2)}) copy-start(s32[12]{0:T(128)S(1)} %compare_select_fusion) | copy-start | bytes 148
  3.7 26.5 %all-to-all-start = ((s32[32,1,2]{2,1,0:T(1,128)}), s32[32,1,2]{2,1,0:T(1,128)S(1)}, u32[]{:S(2)}, u32[]{:S(2)}) async-start(s32[32,1,2]{2,1,0:T(1,128)} %bitcast.2), calls=%async_computation | async-start | bytes 32768 | tf_op jit(solution)/shard_map/all_to_all | solution.py:39
  30.2 7.6 %copy-start.3 = (u32[256]{0:T(256)S(1)}, u32[256]{0:T(256)}, u32[]{:S(2)}) copy-start(u32[256]{0:T(256)} %constant.28) | copy-start | bytes 3076
  30.2 270.6 %all-to-all-start.1 = ((bf16[32,2,128,1152]{3,2,1,0:T(8,128)(2,1)}), bf16[32,2,128,1152]{3,2,1,0:T(8,128)(2,1)}, u32[]{:S(2)}, u32[]{:S(2)}) async-start(bf16[32,2,128,1152]{3,2,1,0:T(8,128)(2,1)} %bitcast.41), calls=%async_computation.1 | async-start | bytes 37748736 | tf_op jit(solution)/shard_map/all_to_all | solution.py:38
  37.7 297.2 %copy-start = (f32[1,576]{1,0:T(1,128)S(1)}, f32[1,576]{1,0:T(1,128)}, u32[]{:S(2)}) copy-start(f32[1,576]{1,0:T(1,128)} %param.10) | copy-start | bytes 6916
  37.7 297.2 %copy-start.1 = (f32[1,576]{1,0:T(1,128)S(1)}, f32[1,576]{1,0:T(1,128)}, u32[]{:S(2)}) copy-start(f32[1,576]{1,0:T(1,128)} %param.11) | copy-start | bytes 6916
where the time goes:
time: 753 us; the launch traced here: 752 us
  blocking collectives  396 us (53%)
  waiting for transfers between devices  261 us (35%)
  matrix products  37.2 us (5%)
  other arithmetic  19.4 us (3%)
  local copies, waits for them, and re-layouts  17.6 us (2%)
  starting transfers between devices  16.1 us (2%)
    all_to_all x1, waiting for transfers between devices, on_device(): lax.all_to_all(send_blocks, 'block', split_axis=0, concat_axis=0, tiled=T...  261 us
    psum x2, blocking collectives, global_norm(): return lax.psum(jnp.sum(residual * scaled_res), ('group', 'block'))  207 us
    psum x1, blocking collectives, on_device(): lax.psum(jnp.sum(direction * operator_image), ('group', 'block'))  85.8 us
    unnamed x3, blocking collectives  66.6 us
    all_gather x2, blocking collectives, on_device(): panel_low = lax.all_gather(low_field, 'group', axis=0, tiled=True)  36.1 us
    dot_general x2, matrix products, on_device(): jnp.einsum('src,sc->sr', got_blocks, inputs, preferred_element_type=jnp.f...  20.3 us
    dot_general x2, matrix products, on_device(): jnp.einsum('src,sr->sc', got_blocks, projected, preferred_element_type=jn...  15.7 us
  transfers between devices with their start and end apart: 2, of which 1 were waited for; matrix products, arithmetic and copies ran while one was open for 3% of the time, Pallas kernels for 0%

commit v1 on v0

--- a/solution.py
+++ b/solution.py
@@ -4,6 +4,19 @@
 from jax.sharding import PartitionSpec as P
 
 ITERS = 2
+
+
+def collect(array, axis, dim):
+    ways = lax.axis_size(axis)
+    up = [(d, (d + 1) % ways) for d in range(ways)]
+    down = [(d, (d - 1) % ways) for d in range(ways)]
+    earlier, later = ([array], [array])
+    for _ in range(ways // 2):
+        earlier.append(lax.ppermute(earlier[-1], axis, up))
+    for _ in range((ways - 1) // 2):
+        later.append(lax.ppermute(later[-1], axis, down))
+    line = jnp.concatenate([*earlier[::-1], *later[1:]], axis=dim)
+    return jnp.roll(line, (lax.axis_index(axis) - ways // 2) * array.shape[dim], axis=dim)
 
 
 def global_norm(residual, scaled_res):
@@ -66,7 +79,7 @@
     precond_norm = global_norm(residual, scaled_res)
     for iteration in range(ITERS):
         low_field = direction.astype(jnp.bfloat16)
-        panel_low = lax.all_gather(low_field, "group", axis=0, tiled=True)
+        panel_low = collect(low_field, "group", 0)
         far_inputs = jnp.dot(selector_low, panel_low, preferred_element_type=jnp.float32).astype(
             jnp.bfloat16
         )

time: 753 us -> 742 us (0.985)
  blocking collectives: 396 us -> 355 us
  starting transfers between devices: 16.1 us -> 32.3 us
  waiting for transfers between devices: 261 us -> 274 us
    all_gather x2 -> x0, blocking collectives: 36.1 us -> none  [on_device(): panel_low = lax.all_gather(low_field, 'group', axis=0, tiled=True)]
    ppermute x0 -> x14, starting transfers between devices: none -> 16.2 us  [the longest x6 15.1 us: collect(): later.append(lax.ppermute(later[-1], axis, down))]
    ppermute x0 -> x14, waiting for transfers between devices: none -> 13.2 us  [the longest x8 13.2 us: collect(): earlier.append(lax.ppermute(earlier[-1], axis, up))]
  transfers between devices with their start and end apart: 2 -> 16, of which waited for: 1 -> 9; matrix products, arithmetic and copies ran while one was open for 3% -> 3% of each run, Pallas kernels for 0% -> 0%
where the time goes in v1:
time: 742 us; the launch traced here: 741 us
  blocking collectives  355 us (48%)
  waiting for transfers between devices  274 us (37%)
  matrix products  37.2 us (5%)
  starting transfers between devices  32.3 us (4%)
  other arithmetic  19.4 us (3%)
  local copies, waits for them, and re-layouts  17.7 us (2%)
    all_to_all x1, waiting for transfers between devices, on_device(): lax.all_to_all(send_blocks, 'block', split_axis=0, concat_axis=0, tiled=T...  261 us
    psum x2, blocking collectives, global_norm(): return lax.psum(jnp.sum(residual * scaled_res), ('group', 'block'))  206 us
    psum x1, blocking collectives, on_device(): lax.psum(jnp.sum(direction * operator_image), ('group', 'block'))  83.8 us
    unnamed x3, blocking collectives  65.9 us
    dot_general x2, matrix products, on_device(): jnp.einsum('src,sc->sr', got_blocks, inputs, preferred_element_type=jnp.f...  20.3 us
    dot_general x2, matrix products, on_device(): jnp.einsum('src,sr->sc', got_blocks, projected, preferred_element_type=jn...  15.7 us
    ppermute x6, starting transfers between devices, collect(): later.append(lax.ppermute(later[-1], axis, down))  15.1 us
  transfers between devices with their start and end apart: 16, of which 9 were waited for; matrix products, arithmetic and copies ran while one was open for 3% of the time, Pallas kernels for 0%

profile of v1, /device:TPU:1, one launch (start us, length us, event | category | flops | bytes accessed | tf_op | source)
XLA Modules:
  0.0 741.3 jit_solution(4823526198756674383)
XLA Ops:
  3.7 8.6 %all-to-all-start = ((s32[32,1,2]{2,1,0:T(1,128)}), s32[32,1,2]{2,1,0:T(1,128)S(1)}, u32[]{:S(2)}, u32[]{:S(2)}) async-start(s32[32,1,2]{2,1,0:T(1,128)} %bitcast.2), calls=%async_computation | async-start | bytes 32768 | tf_op jit(solution)/shard_map/all_to_all | solution.py:52
  13.0 2.3 broadcast_select_fusion
  15.3 7.1 broadcast_in_dim.26
  22.4 7.7 %scatter_fusion = bf16[64,128,1152]{2,1,0:T(8,128)(2,1)} fusion(bf16[64,128,1152]{2,1,0:T(8,128)(2,1)} %broadcast_in_dim.26, s32[12]{0:T(128)} %copy-done.2, bf16[12,128,1152]{2,1,0:T(8,128)(2,1)S(1)} %broadcast_select_fusion), kind=kCustom, calls=%fused_computation.1 | custom fusion | bytes 10616880 | tf_op jit(solution)/shard_map/scatter | solution.py:45
  30.2 7.5 %all-to-all-start.1 = ((bf16[32,2,128,1152]{3,2,1,0:T(8,128)(2,1)}), bf16[32,2,128,1152]{3,2,1,0:T(8,128)(2,1)}, u32[]{:S(2)}, u32[]{:S(2)}) async-start(bf16[32,2,128,1152]{3,2,1,0:T(8,128)(2,1)} %bitcast.31), calls=%async_computation.1 | async-start | bytes 37748736 | tf_op jit(solution)/shard_map/all_to_all | solution.py:51
  39.6 261.2 %all-to-all-done.1 = bf16[32,2,128,1152]{3,2,1,0:T(8,128)(2,1)} async-done(((bf16[32,2,128,1152]{3,2,1,0:T(8,128)(2,1)}), bf16[32,2,128,1152]{3,2,1,0:T(8,128)(2,1)}, u32[]{:S(2)}, u32[]{:S(2)}) %all-to-all-start.1) | async-done | bytes 18874400 | tf_op jit(solution)/shard_map/all_to_all | solution.py:51
  300.8 8.3 %fusion = f32[64,1152]{1,0:T(8,128)S(1)} fusion(bf16[32,2,128,1152]{3,2,1,0:T(8,128)(2,1)} %all-to-all-done.1), kind=kLoop, calls=%fused_computation.3 | loop fusion | flops 28237824 | bytes 19169280 | tf_op jit(solution)/shard_map/src,src->sc/dot_general | solution.py:71
  309.4 25.5 %all-reduce = f32[8,576]{1,0:T(8,128)S(1)} all-reduce(f32[8,576]{1,0:T(8,128)S(1)} %convolution_add_fusion.2), channel_id=2, replica_groups=mesh['group'=8,'block'=32] {'group'}, use_global_device_ids=true, to_apply=%region_4.5.clone | all-reduce | flops 4608 | bytes 36864
  335.7 2.7 collective-permute-start.4
  339.3 2.7 collective-permute-start.5
  343.0 2.7 collective-permute-start.6
  346.6 3.6 collective-permute-done.3
  350.6 10.1 %fusion.3 = f32[64,1,128]{2,1,0:T(1,128)S(1)} fusion(bf16[64,128,1152]{2,1,0:T(8,128)(2,1)} %bitcast.4, bf16[64,1152,1]{1,0,2:T(8,128)(2,1)S(1)} %maximum_bitcast_fusion), kind=kOutput, calls=%fused_computation.14 | convolution fusion | flops 18874368 | bytes 19054592 | tf_op jit(solution)/shard_map/src,sc->sr/dot_general | solution.py:88
  360.8 7.8 %fusion.10 = f32[64,1,1152]{2,1,0:T(1,128)S(1)} fusion(bf16[64,128,1152]{2,1,0:T(8,128)(2,1)} %bitcast.4, bf16[64,128,1]{1,0,2:T(8,128)(2,1)S(1)} %convert_bitcast_fusion.1), kind=kOutput, calls=%fused_computation.26 | convolution fusion | flops 18874368 | bytes 19185664 | tf_op jit(solution)/shard_map/src,sr->sc/dot_general | solution.py:91
  369.0 20.1 %all-reduce.1 = f32[8,576]{1,0:T(8,128)S(1)} all-reduce(f32[8,576]{1,0:T(8,128)S(1)} %convolution_add_fusion.1), channel_id=3, replica_groups=mesh['group'=8,'block'=32] {'group'}, use_global_device_ids=true, to_apply=%region_8.10.clone | all-reduce | flops 4608 | bytes 36864
  390.3 132.3 %all-reduce.3 = (f32[]{:T(128)}, f32[]{:T(128)}) all-reduce(f32[]{:T(128)} %get-tuple-element.4, f32[]{:T(128)} %get-tuple-element.3), channel_id=1, replica_groups=mesh['group'=8,'block'=32] {'group','block'}, use_global_device_ids=true, to_apply=%region_6.7 | all-reduce | flops 2 | bytes 16 | tf_op jit(solution)/shard_map/psum | solution.py:23
  525.2 73.4 %psum.30 = f32[]{:T(128)} all-reduce(f32[]{:T(128)} %get-tuple-element.9), channel_id=1, replica_groups=mesh['group'=8,'block'=32] {'group','block'}, use_global_device_ids=true, to_apply=%region_12.14 | all-reduce | flops 1 | bytes 8 | tf_op jit(solution)/shard_map/psum | solution.py:23
  603.7 2.7 collective-permute-start.12
  607.4 2.7 collective-permute-start.13
  611.1 3.7 collective-permute-done.10
  615.1 10.1 %fusion.1 = f32[64,1,128]{2,1,0:T(1,128)S(1)} fusion(bf16[64,128,1152]{2,1,0:T(8,128)(2,1)} %bitcast.4, bf16[64,1152,1]{1,0,2:T(8,128)(2,1)S(1)} %maximum_bitcast_fusion.1), kind=kOutput, calls=%fused_computation.11 | convolution fusion | flops 18874368 | bytes 19054592 | tf_op jit(solution)/shard_map/src,sc->sr/dot_general | solution.py:88
  625.3 7.8 %fusion.8 = f32[64,1,1152]{2,1,0:T(1,128)S(1)} fusion(bf16[64,128,1152]{2,1,0:T(8,128)(2,1)} %bitcast.4, bf16[64,128,1]{1,0,2:T(8,128)(2,1)S(1)} %convert_bitcast_fusion), kind=kOutput, calls=%fused_computation.24 | convolution fusion | flops 18874368 | bytes 19185664 | tf_op jit(solution)/shard_map/src,sr->sc/dot_general | solution.py:91
  633.4 20.2 %all-reduce.2 = f32[8,576]{1,0:T(8,128)S(1)} all-reduce(f32[8,576]{1,0:T(8,128)S(1)} %convolution_add_fusion), channel_id=4, replica_groups=mesh['group'=8,'block'=32] {'group'}, use_global_device_ids=true, to_apply=%region_14.16.clone | all-reduce | flops 4608 | bytes 36864
  654.9 83.8 %psum.31 = f32[]{:T(128)} all-reduce(f32[]{:T(128)} %multiply_reduce_fusion), channel_id=1, replica_groups=mesh['group'=8,'block'=32] {'group','block'}, use_global_device_ids=true, to_apply=%region_16.18 | all-reduce | flops 1 | bytes 8 | tf_op jit(solution)/shard_map/psum | solution.py:97
  (66 shorter events, 21.7 us)
Async XLA Ops:
  2.2 10.0 %copy-start.2 = (s32[12]{0:T(128)}, s32[12]{0:T(128)S(1)}, u32[]{:S(2)}) copy-start(s32[12]{0:T(128)S(1)} %compare_select_fusion) | copy-start | bytes 148
  3.7 26.5 %all-to-all-start = ((s32[32,1,2]{2,1,0:T(1,128)}), s32[32,1,2]{2,1,0:T(1,128)S(1)}, u32[]{:S(2)}, u32[]{:S(2)}) async-start(s32[32,1,2]{2,1,0:T(1,128)} %bitcast.2), calls=%async_computation | async-start | bytes 32768 | tf_op jit(solution)/shard_map/all_to_all | solution.py:52
  30.2 7.6 %copy-start.3 = (u32[256]{0:T(256)S(1)}, u32[256]{0:T(256)}, u32[]{:S(2)}) copy-start(u32[256]{0:T(256)} %constant.48) | copy-start | bytes 3076
  30.2 270.6 %all-to-all-start.1 = ((bf16[32,2,128,1152]{3,2,1,0:T(8,128)(2,1)}), bf16[32,2,128,1152]{3,2,1,0:T(8,128)(2,1)}, u32[]{:S(2)}, u32[]{:S(2)}) async-start(bf16[32,2,128,1152]{3,2,1,0:T(8,128)(2,1)} %bitcast.31), calls=%async_computation.1 | async-start | bytes 37748736 | tf_op jit(solution)/shard_map/all_to_all | solution.py:51
  37.7 297.2 %copy-start = (f32[1,576]{1,0:T(1,128)S(1)}, f32[1,576]{1,0:T(1,128)}, u32[]{:S(2)}) copy-start(f32[1,576]{1,0:T(1,128)} %param.12) | copy-start | bytes 6916
  37.7 297.2 %copy-start.1 = (f32[1,576]{1,0:T(1,128)S(1)}, f32[1,576]{1,0:T(1,128)}, u32[]{:S(2)}) copy-start(f32[1,576]{1,0:T(1,128)} %param.13) | copy-start | bytes 6916
  335.6 3.7 collective-permute-start
  335.7 3.6 collective-permute-start.4
  339.3 3.7 collective-permute-start.1
  339.3 3.7 collective-permute-start.5
  343.0 3.7 collective-permute-start.2
  343.0 3.7 collective-permute-start.6
  346.6 3.7 collective-permute-start.3
  600.0 3.7 collective-permute-start.7
  601.0 2.8 collective-permute-start.11
  603.7 3.7 collective-permute-start.8
  603.7 3.7 collective-permute-start.12
  607.4 3.7 collective-permute-start.9
  607.4 3.7 collective-permute-start.13
  611.0 3.7 collective-permute-start.10
